TPU v7x, 32 devices: a whole 2x2x4 slice. The times are simulated.
32 devices in a mesh: ctx: 4 (over y, x), ch: 8 (over z, core).
Axes of the slice: x: 2, y: 2, z: 4, core: 2. Of those that a mesh axis runs over, the one named last changes fastest.
Arguments:
- queries: bfloat16 [4096, 4096], P('ctx', 'ch'), may hold values from -12 to 12
- key_input: bfloat16 [4096, 4096], P('ctx', 'ch'), may hold values from -6 to 6
- value_input: bfloat16 [4096, 4096], P('ctx', 'ch'), may hold values from -6 to 6
- filters: bfloat16 [4096, 4096], P('ctx', 'ch'), may hold values from -0.3 to 0.3
- skip_gain: float32 [4096], P('ch'), may hold values from -0.3 to 0.3
- out_weight: bfloat16 [4096, 4096], P('ch'), may hold values from -0.125 to 0.125
Outputs:
- layer_out: bfloat16 [4096, 4096], P('ctx', 'ch')
All inputs are finite; a program needn't handle non-finite values.
Results may differ from a plain program's by a relative error of at most 0.019.
Values may be sent and summed in bfloat16 or wider, within the bound.
A program may use at most 320 MiB of HBM per device.

v0:
```python
import functools

import jax
import jax.numpy as jnp
import numpy as np
from jax import lax
from jax.experimental import pallas as pl
from jax.experimental.pallas import tpu as pltpu
from jax.sharding import PartitionSpec as P

BLOCK = 256
F32 = jnp.float32
BF16 = jnp.bfloat16


def transform_tables(block):
    k = np.arange(block)[:, None]
    n = np.arange(block)[None, :]
    angle = np.pi * (((2 * k + 1) * n) % (4 * block)) / (2 * block)
    forward = np.concatenate([np.cos(angle), -np.sin(angle)], axis=0)
    backward = np.concatenate([np.cos(angle).T, -np.sin(angle).T], axis=1) / block

    def halves(table):
        high = table.astype(BF16)
        low = (table - high.astype(np.float64)).astype(BF16)
        return high, low

    f_high, f_low = halves(forward)
    b_high, b_low = halves(backward)
    return np.stack([f_high, f_low]), np.stack([b_high, b_low])


def dot(left, right):
    return jnp.dot(left, right, preferred_element_type=F32)


MESH = pl.DeviceIdType.MESH


def gate_kernel(n_ctx, q_ref, k_ref, v_ref, h_ref, skip_ref, f_ref, b_ref, w_ref, out_ref, wx,
                outbox, inbox, spec, prod, conv_out, conv_in,
                w_send, w_recv, in_send, in_recv, back_send, back_recv):
    me = lax.axis_index("ctx")
    ch = lax.axis_index("ch")
    core = lax.rem(ch, 2)
    mate = ch + 1 - 2 * core
    n_chip, _, wide = wx.shape
    tokens = q_ref.shape[0]
    width = conv_in.shape[2]
    block = BLOCK
    per = tokens // block
    nb = n_ctx * per

    barrier = pltpu.get_barrier_semaphore()
    pl.semaphore_signal(barrier, inc=1, device_id={"ch": mate}, device_id_type=MESH)
    for d in range(1, n_ctx):
        pl.semaphore_signal(
            barrier, inc=1, device_id={"ctx": lax.rem(me + d, n_ctx)}, device_id_type=MESH
        )

    def rows_of(r):
        return pl.ds(pl.multiple_of(r * block, block), block)

    def fill(r, carry):
        at = rows_of(r)
        for i in range(n_ctx):
            lanes = slice(i * width, (i + 1) * width)
            mixed = k_ref[at, lanes].astype(F32) * v_ref[at, lanes].astype(F32)
            outbox[i, at, :width] = mixed.astype(BF16)
            outbox[i, at, width:] = h_ref[at, lanes]
        return carry

    lax.fori_loop(0, per, fill, 0)
    pl.semaphore_wait(barrier, n_ctx)

    def in_copy(d):
        to = lax.rem(me + d, n_ctx)
        return pltpu.make_async_remote_copy(
            src_ref=outbox.at[to], dst_ref=inbox.at[me],
            send_sem=in_send.at[d], recv_sem=in_recv.at[d],
            device_id={"ctx": to}, device_id_type=MESH,
        )

    def in_wait(d):
        source = lax.rem(me + n_ctx - d, n_ctx)
        pltpu.make_async_remote_copy(
            src_ref=outbox.at[source], dst_ref=inbox.at[source],
            send_sem=in_send.at[d], recv_sem=in_recv.at[d],
            device_id={"ctx": source}, device_id_type=MESH,
        ).wait_recv()

    def back_copy(d):
        to = lax.rem(me + d, n_ctx)
        return pltpu.make_async_remote_copy(
            src_ref=conv_out.at[to], dst_ref=conv_in.at[me],
            send_sem=back_send.at[d], recv_sem=back_recv.at[d],
            device_id={"ctx": to}, device_id_type=MESH,
        )

    def back_wait(d):
        source = lax.rem(me + n_ctx - d, n_ctx)
        pltpu.make_async_remote_copy(
            src_ref=conv_out.at[source], dst_ref=conv_in.at[source],
            send_sem=back_send.at[d], recv_sem=back_recv.at[d],
            device_id={"ctx": source}, device_id_type=MESH,
        ).wait_recv()

    def w_copy(t):
        lanes = pl.ds(pl.multiple_of((t * 2 + 1 - core) * wide, wide), wide)
        return pltpu.make_async_remote_copy(
            src_ref=w_ref.at[:, lanes], dst_ref=wx.at[t],
            send_sem=w_send.at[t], recv_sem=w_recv.at[t],
            device_id={"ch": mate}, device_id_type=MESH,
        )

    for d in range(1, n_ctx):
        in_copy(d).start()
    for t in range(n_chip):
        w_copy(t).start()

    def ahead(box, source):
        def one(r, carry):
            data = box[source, rows_of(r), :]
            spec[source * per + r] = dot(f_ref[0], data) + dot(f_ref[1], data)
            return carry

        lax.fori_loop(0, per, one, 0)

    ahead(outbox, me)
    for d in range(1, n_ctx):
        in_wait(d)
        ahead(inbox, lax.rem(me + n_ctx - d, n_ctx))

    rows = 8
    sign = 1.0 - 2.0 * (lax.broadcasted_iota(jnp.int32, (rows, width), 0) % 2).astype(F32)

    def products(chunk, carry):
        top = pl.multiple_of(chunk * rows, rows)
        re = pl.ds(top, rows)
        im = pl.ds(pl.multiple_of(block + top, rows), rows)
        x = [(spec[p, re, :width], spec[p, im, :width]) for p in range(nb)]
        h = [(spec[p, re, width:], spec[p, im, width:]) for p in range(nb)]
        last = None
        for j in range(nb):
            zr = zi = None
            for p in range(j + 1):
                xr, xi = x[p]
                hr, hi = h[j - p]
                tr = xr * hr - xi * hi
                ti = xr * hi + xi * hr
                zr = tr if zr is None else zr + tr
                zi = ti if zi is None else zi + ti
            if last is None:
                yr, yi = zr, zi
            else:
                yr = zr - sign * last[1]
                yi = zi + sign * last[0]
            last = (zr, zi)
            prod[j, re, :] = yr
            prod[j, im, :] = yi
        return carry

    lax.fori_loop(0, block // rows, products, 0)

    def back(box, to):
        def one(r, carry):
            j = to * per + 2 * r
            data = jnp.concatenate([prod[j], prod[j + 1]], axis=1)
            high = data.astype(BF16)
            low = (data - high.astype(F32)).astype(BF16)
            conv = (dot(b_ref[0], high) + (dot(b_ref[0], low) + dot(b_ref[1], high))).astype(BF16)
            box[to, rows_of(2 * r), :] = conv[:, :width]
            box[to, rows_of(2 * r + 1), :] = conv[:, width:]
            return carry

        lax.fori_loop(0, per // 2, one, 0)

    for d in range(1, n_ctx):
        back(conv_out, lax.rem(me + d, n_ctx))
        back_copy(d).start()
    back(conv_in, me)
    for d in range(1, n_ctx):
        back_wait(d)

    def gate(r, carry):
        at = rows_of(r)
        for i in range(n_ctx):
            lanes = slice(i * width, (i + 1) * width)
            mixed = outbox[i, at, :width].astype(F32)
            total = conv_in[i, at, :].astype(F32) + skip_ref[:, lanes] * mixed
            out_ref[at, lanes] = (q_ref[at, lanes].astype(F32) * total).astype(BF16)
        return carry

    lax.fori_loop(0, per, gate, 0)
    for d in range(1, n_ctx):
        in_copy(d).wait_send()
        back_copy(d).wait_send()
    for t in range(n_chip):
        w_copy(t).wait()


def gated_conv(queries, key_input, value_input, filters, skip_gain, out_weight):
    tokens, channels = queries.shape
    n_ctx = lax.axis_size("ctx")
    n_ch = lax.axis_size("ch")
    n_chip = n_ch // 2
    width = channels // n_ctx
    nb = n_ctx * tokens // BLOCK
    forward, backward = transform_tables(BLOCK)
    vmem = pl.BlockSpec(memory_space=pltpu.VMEM)
    hbm = pl.BlockSpec(memory_space=pl.ANY)
    return pl.pallas_call(
        functools.partial(gate_kernel, n_ctx),
        out_shape=(
            jax.ShapeDtypeStruct((tokens, channels), BF16),
            jax.ShapeDtypeStruct((n_chip, channels, out_weight.shape[1] // n_ch), BF16),
        ),
        in_specs=[vmem] * 7 + [hbm],
        out_specs=(vmem, hbm),
        scratch_shapes=[
            pltpu.VMEM((n_ctx, tokens, 2 * width), BF16),
            pltpu.VMEM((n_ctx, tokens, 2 * width), BF16),
            pltpu.VMEM((nb, 2 * BLOCK, 2 * width), F32),
            pltpu.VMEM((nb, 2 * BLOCK, width), F32),
            pltpu.VMEM((n_ctx, tokens, width), BF16),
            pltpu.VMEM((n_ctx, tokens, width), BF16),
            pltpu.SemaphoreType.DMA((n_chip,)),
            pltpu.SemaphoreType.DMA((n_chip,)),
            pltpu.SemaphoreType.DMA((n_ctx,)),
            pltpu.SemaphoreType.DMA((n_ctx,)),
            pltpu.SemaphoreType.DMA((n_ctx,)),
            pltpu.SemaphoreType.DMA((n_ctx,)),
        ],
        compiler_params=pltpu.CompilerParams(
            collective_id=1, has_side_effects=True, vmem_limit_bytes=56 * 1024 * 1024
        ),
        cost_estimate=pl.CostEstimate(
            flops=28 * n_ctx * tokens * BLOCK * width, bytes_accessed=10 * tokens * channels,
            transcendentals=0,
        ),
    )(queries, key_input, value_input, filters, skip_gain[None, :],
      jnp.asarray(forward), jnp.asarray(backward), out_weight)


CHUNKS = 4


def project_kernel(n_ch, g_ref, w_ref, wx, out_ref, w_own, w_sem, gx, send, from_left, from_right, own,
                   g_send, g_recv, send_sem, left_sem, right_sem):
    me = lax.axis_index("ch")
    chip = lax.div(me, 2)
    core = lax.rem(me, 2)
    mate = chip * 2 + 1 - core
    n_chip = n_ch // 2
    tokens, block = out_ref.shape
    rows = tokens // CHUNKS
    has_left = chip > 0
    has_right = chip < n_chip - 1
    left = jnp.maximum(me - 2, core)
    right = jnp.minimum(me + 2, n_ch - 2 + core)

    def w_load(t):
        lanes = pl.ds(pl.multiple_of((t * 2 + core) * block, block), block)
        return pltpu.make_async_copy(w_ref.at[:, lanes], w_own.at[t], w_sem.at[t])

    for t in range(n_chip):
        w_load(t).start()

    barrier = pltpu.get_barrier_semaphore()
    pl.semaphore_signal(barrier, inc=1, device_id={"ch": mate}, device_id_type=MESH)

    @pl.when(has_left)
    def _():
        pl.semaphore_signal(barrier, inc=1, device_id={"ch": left}, device_id_type=MESH)

    @pl.when(has_right)
    def _():
        pl.semaphore_signal(barrier, inc=1, device_id={"ch": right}, device_id_type=MESH)

    pl.semaphore_wait(barrier, 1 + has_left.astype(jnp.int32) + has_right.astype(jnp.int32))

    def columns(chip_at, core_at):
        return pl.ds(pl.multiple_of((chip_at * 2 + core_at) * block, block), block)

    def tokens_of(m):
        return pl.ds(pl.multiple_of(m * rows, rows), rows)

    def remote(src, dst, sent, arrived, target):
        return pltpu.make_async_remote_copy(
            src_ref=src, dst_ref=dst, send_sem=sent, recv_sem=arrived,
            device_id={"ch": target}, device_id_type=MESH,
        )

    def g_copy(m):
        at = tokens_of(m)
        return remote(g_ref.at[at], gx.at[at], g_send.at[m], g_recv.at[m], mate)

    def to_right(t, m):
        at = tokens_of(m)
        return remote(send.at[t, at], from_left.at[t, at], send_sem.at[t, m], left_sem.at[t, m], right)

    def to_left(t, m):
        at = tokens_of(m)
        return remote(send.at[t, at], from_right.at[t, at], send_sem.at[t, m], right_sem.at[t, m], left)

    def arrive_left(t, m):
        at = tokens_of(m)
        return remote(send.at[t, at], from_left.at[t, at], send_sem.at[t, m], left_sem.at[t, m], left)

    def arrive_right(t, m):
        at = tokens_of(m)
        return remote(send.at[t, at], from_right.at[t, at], send_sem.at[t, m], right_sem.at[t, m], right)

    for m in range(CHUNKS):
        g_copy(m).start()

    for t in range(n_chip):
        w_load(t).wait()

    def share(t, m):
        at = tokens_of(m)
        return dot(g_ref[at, :], w_own[t]) + dot(gx[at, :], wx[t])

    def pass_on(t, m, first, arrived, copy):
        at = tokens_of(m)
        part = share(t, m)

        @pl.when(first)
        def _():
            send[t, at, :] = part.astype(BF16)

        @pl.when(jnp.logical_not(first))
        def _():
            arrived(t, m)

        @pl.when(jnp.logical_not(first))
        def _():
            buffer = from_left if copy is to_right else from_right
            send[t, at, :] = (part + buffer[t, at, :].astype(F32)).astype(BF16)

        copy(t, m).start()

    def drain(m):
        for d in range(n_chip - 1, 0, -1):
            @pl.when(chip + d < n_chip)
            def _():
                to_right(chip + d, m).wait_send()

            @pl.when(chip - d >= 0)
            def _():
                to_left(chip - d, m).wait_send()

    def step(m, carry):
        g_copy(m).wait()

        @pl.when(m >= 2)
        def _():
            drain(m - 2)

        for d in range(n_chip - 1, 0, -1):
            @pl.when(chip + d < n_chip)
            def _():
                pass_on(chip + d, m, jnp.logical_not(has_left),
                        lambda t, m: arrive_left(t, m).wait_recv(), to_right)

            @pl.when(chip - d >= 0)
            def _():
                pass_on(chip - d, m, jnp.logical_not(has_right),
                        lambda t, m: arrive_right(t, m).wait_recv(), to_left)

        own[tokens_of(m), :] = share(chip, m)
        return carry

    lax.fori_loop(0, CHUNKS, step, 0)

    def finish(m, carry):
        at = tokens_of(m)

        @pl.when(has_left)
        def _():
            arrive_left(chip, m).wait_recv()
            own[at, :] += from_left[chip, at, :].astype(F32)

        @pl.when(has_right)
        def _():
            arrive_right(chip, m).wait_recv()
            own[at, :] += from_right[chip, at, :].astype(F32)

        out_ref[at, :] = own[at, :].astype(BF16)
        return carry

    lax.fori_loop(0, CHUNKS, finish, 0)
    drain(CHUNKS - 2)
    drain(CHUNKS - 1)


def project(gated, out_weight, mate_weight):
    tokens, channels = gated.shape
    n_ch = lax.axis_size("ch")
    n_chip = n_ch // 2
    block = out_weight.shape[1] // n_ch
    return pl.pallas_call(
        functools.partial(project_kernel, n_ch),
        out_shape=jax.ShapeDtypeStruct((tokens, block), BF16),
        in_specs=[
            pl.BlockSpec(memory_space=pltpu.VMEM),
            pl.BlockSpec(memory_space=pl.ANY),
            pl.BlockSpec(memory_space=pltpu.VMEM),
        ],
        out_specs=pl.BlockSpec(memory_space=pltpu.VMEM),
        scratch_shapes=[
            pltpu.VMEM((n_chip, channels, block), BF16),
            pltpu.SemaphoreType.DMA((n_chip,)),
            pltpu.VMEM((tokens, channels), BF16),
            pltpu.VMEM((n_chip, tokens, block), BF16),
            pltpu.VMEM((n_chip, tokens, block), BF16),
            pltpu.VMEM((n_chip, tokens, block), BF16),
            pltpu.VMEM((tokens, block), F32),
            pltpu.SemaphoreType.DMA((CHUNKS,)),
            pltpu.SemaphoreType.DMA((CHUNKS,)),
            pltpu.SemaphoreType.DMA((n_chip, CHUNKS)),
            pltpu.SemaphoreType.DMA((n_chip, CHUNKS)),
            pltpu.SemaphoreType.DMA((n_chip, CHUNKS)),
        ],
        compiler_params=pltpu.CompilerParams(
            collective_id=0, has_side_effects=True, vmem_limit_bytes=48 * 1024 * 1024
        ),
        cost_estimate=pl.CostEstimate(
            flops=2 * tokens * channels * n_ch * block,
            bytes_accessed=2 * channels * n_ch * block, transcendentals=0,
        ),
    )(gated, out_weight, mate_weight)


def per_device(queries, key_input, value_input, filters, skip_gain, out_weight):
    gated, mate_weight = gated_conv(
        queries, key_input, value_input, filters, skip_gain, out_weight
    )
    return project(gated, out_weight, mate_weight)


def solution(mesh):
    in_specs = (
        P("ctx", "ch"),
        P("ctx", "ch"),
        P("ctx", "ch"),
        P("ctx", "ch"),
        P("ch"),
        P("ch", None),
    )
    return jax.shard_map(
        per_device, mesh=mesh, in_specs=in_specs, out_specs=P("ctx", "ch"), check_vma=False
    )
```

profile of v0, /device:TPU:10, one launch (start us, length us, event | category | flops | bytes accessed | tf_op | source)
XLA Modules:
  0.0 131.8 jit_solution(11921819182328567715)
XLA Ops:
  0.0 52.0 %shard_map.82 = (bf16[1024,512]{1,0:T(8,128)(2,1)}, bf16[4,512,512]{2,1,0:T(8,128)(2,1)}) custom-call(bf16[1024,512]{1,0:T(8,128)(2,1)} %q_ref.1, bf16[1024,512]{1,0:T(8,128)(2,1)} %k_ref.1, bf16[1024,512]{1,0:T(8,128)(2,1)} %v_ref.1, bf16[1024,512]{1,0:T(8,128)(2,1)} %h_ref.1, f32[1,512]{1,0:T(1,128)} %bitcast.1, bf16[2,512,256]{2,1,0:T(8,128)(2,1)} %constant.4.clone.f_ref, ...), custom_call_target="tpu_custom_call" | custom-call | flops 3758096384 | bytes 5242880 | tf_op jit(solution)/shard_map/pallas_call | solution.py:212
  52.1 0.0 copy-start
  52.1 1.6 %copy-done = bf16[4,512,512]{2,1,0:T(8,128)(2,1)S(1)} copy-done((bf16[4,512,512]{2,1,0:T(8,128)(2,1)S(1)}, bf16[4,512,512]{2,1,0:T(8,128)(2,1)}, u32[]{:S(2)}) %copy-start) | copy-done | bytes 2097176
  53.6 0.0 copy-start.1
  53.6 1.2 copy-done.1
  54.9 75.9 %shard_map.83 = bf16[1024,512]{1,0:T(8,128)(2,1)S(1)} custom-call(bf16[1024,512]{1,0:T(8,128)(2,1)S(1)} %copy-done.1, bf16[512,4096]{1,0:T(8,128)(2,1)} %w_ref.3, bf16[4,512,512]{2,1,0:T(8,128)(2,1)S(1)} %copy-done), custom_call_target="tpu_custom_call" | custom-call | flops 4294967296 | bytes 4194304 | tf_op jit(solution)/shard_map/pallas_call | solution.py:402
  130.8 1.0 copy.10
Async XLA Ops:
  52.1 1.6 %copy-start = (bf16[4,512,512]{2,1,0:T(8,128)(2,1)S(1)}, bf16[4,512,512]{2,1,0:T(8,128)(2,1)}, u32[]{:S(2)}) copy-start(bf16[4,512,512]{2,1,0:T(8,128)(2,1)} %get-tuple-element.8.wx) | copy-start | bytes 6291460
  53.6 1.2 copy-start.1
where the time goes:
time: 133 us; the launch traced here: 132 us
  Pallas kernels  128 us (96%)
  local copies, waits for them, and re-layouts  3.78 us (3%)
    pallas_call x1, Pallas kernels, project(): pl.pallas_call(functools.partial(project_kernel, n_ch), out_shape=jax.Sha...  75.9 us
    pallas_call x1, Pallas kernels, gated_conv(): pl.pallas_call(functools.partial(gate_kernel, n_ctx), out_shape=(jax.Shap...  52 us
    unnamed x5, local copies, waits for them, and re-layouts  3.78 us

commit v1 on v0

v1 whole, which is shorter than its diff:
```python
import functools

import jax
import jax.numpy as jnp
import numpy as np
from jax import lax
from jax.experimental import pallas as pl
from jax.experimental.pallas import tpu as pltpu
from jax.sharding import PartitionSpec as P

BLOCK = 256
SUB = 128
F32 = jnp.float32
BF16 = jnp.bfloat16


def transform_tables(block):
    k = np.arange(block)[:, None]
    n = np.arange(block)[None, :]
    angle = np.pi * (((2 * k + 1) * n) % (4 * block)) / (2 * block)
    forward = np.concatenate([np.cos(angle), -np.sin(angle)], axis=0)
    backward = np.concatenate([np.cos(angle).T, -np.sin(angle).T], axis=1) / block

    def halves(table):
        high = table.astype(BF16)
        low = (table - high.astype(np.float64)).astype(BF16)
        return high, low

    f_high, f_low = halves(forward)
    b_high, b_low = halves(backward)
    return np.stack([f_high, f_low]), np.stack([b_high, b_low])


def dot(left, right):
    return jnp.dot(left, right, preferred_element_type=F32)


MESH = pl.DeviceIdType.MESH


def layer_kernel(n_ctx, n_ch, relay, q_hbm, k_hbm, v_hbm, h_hbm, skip_ref, f_hbm, b_hbm, w_hbm, out_ref,
                 q_ref, k_ref, v_ref, h_ref, f_ref, b_ref, w_own, wx, we,
                 outbox, inbox, spec, zbuf, ybuf, conv_out, conv_in, g_ref, gx,
                 send_a, send_b, send_c, recv_a, recv_b, recv_c, ge, gex, own,
                 load_sem, table_sem, w_sem, w_send, w_recv, we_send, we_recv, we_fwd,
                 in_send, in_recv, back_send, back_recv, g_send, g_recv,
                 a_send, a_recv, b_send, b_recv, c_send, c_recv, ge_send, ge_recv, gex_send, gex_recv):
    me = lax.axis_index("ctx")
    ch = lax.axis_index("ch")
    chip = lax.div(ch, 2)
    core = lax.rem(ch, 2)
    mate = ch + 1 - 2 * core
    n_chip = n_ch // 2
    tokens, block = out_ref.shape
    width = conv_in.shape[2]
    per = tokens // BLOCK
    has_left = chip > 0
    has_right = chip < n_chip - 1
    left = jnp.maximum(ch - 2, core)
    right = jnp.minimum(ch + 2, n_ch - 2 + core)

    def remote(src, dst, sent, arrived, target):
        return pltpu.make_async_remote_copy(
            src_ref=src, dst_ref=dst, send_sem=sent, recv_sem=arrived,
            device_id=target, device_id_type=MESH,
        )

    def rows_of(r, size=BLOCK):
        return pl.ds(pl.multiple_of(r * size, size), size)

    barrier = pltpu.get_barrier_semaphore()

    def greet(target):
        pl.semaphore_signal(barrier, inc=1, device_id=target, device_id_type=MESH)

    greet({"ch": mate})
    for d in range(1, n_ctx):
        greet({"ctx": lax.rem(me + d, n_ctx)})

    @pl.when(has_left)
    def _():
        greet({"ch": left})
        greet({"ch": left + 1 - 2 * core})

    @pl.when(has_right)
    def _():
        greet({"ch": right})
        greet({"ch": right + 1 - 2 * core})

    def load(a, r):
        source, target = ((k_hbm, k_ref), (v_hbm, v_ref), (h_hbm, h_ref))[a]
        at = rows_of(r)
        return pltpu.make_async_copy(source.at[at], target.at[at], load_sem.at[a, r])

    f_load = pltpu.make_async_copy(f_hbm, f_ref, table_sem.at[0])
    b_load = pltpu.make_async_copy(b_hbm, b_ref, table_sem.at[1])
    q_load = pltpu.make_async_copy(q_hbm, q_ref, table_sem.at[2])

    def lanes_of(chip_at, core_at):
        return pl.ds(pl.multiple_of((chip_at * 2 + core_at) * block, block), block)

    def w_load(t):
        return pltpu.make_async_copy(w_hbm.at[:, lanes_of(t, core)], w_own.at[t], w_sem.at[t])

    def w_copy(t):
        return remote(w_hbm.at[:, lanes_of(t, 1 - core)], wx.at[t], w_send.at[t], w_recv.at[t], {"ch": mate})

    for r in range(per):
        for a in range(3):
            load(a, r).start()
    f_load.start()

    def in_copy(i, r):
        at = rows_of(r)
        return remote(outbox.at[i, at], inbox.at[me, at], in_send.at[i, r], in_recv.at[me, r], {"ctx": i})

    def in_arrival(i, r):
        at = rows_of(r)
        return remote(outbox.at[i, at], inbox.at[i, at], in_send.at[i, r], in_recv.at[i, r], {"ctx": i})

    pl.semaphore_wait(
        barrier, n_ctx + 2 * has_left.astype(jnp.int32) + 2 * has_right.astype(jnp.int32)
    )

    def fill(r, carry):
        for a in range(3):
            load(a, r).wait()
        at = rows_of(r)
        for i in range(n_ctx):
            lanes = slice(i * width, (i + 1) * width)
            mixed = k_ref[at, lanes].astype(F32) * v_ref[at, lanes].astype(F32)
            outbox[i, at, :width] = mixed.astype(BF16)
            outbox[i, at, width:] = h_ref[at, lanes]

            @pl.when(me != i)
            def _():
                in_copy(i, r).start()
        return carry

    lax.fori_loop(0, per, fill, 0)

    low = 1 - lax.div(chip, n_chip // 2)
    is_end = jnp.logical_or(chip == 0, chip == n_chip - 1)
    is_mid = jnp.logical_not(is_end)
    far = (n_chip - 1) * low
    end = (n_chip - 1) * (1 - low)
    across = n_chip - 1 - chip
    inner = 2 - low

    def bit_of(core_at):
        return (1 - core_at) * lax.rem(me, 2) + core_at * lax.div(me, 2)

    bit = bit_of(core)
    partner = (1 - core) * (me + 1 - 2 * lax.rem(me, 2)) + core * lax.rem(me + 2, 4)

    def we_copy(slot, core_at):
        column = inner * (1 - slot) + (n_chip - 1 - inner) * slot
        return remote(w_hbm.at[:, lanes_of(column, core_at)], we.at[slot, core],
                      we_send.at[slot, core_at], we_recv.at[slot, core], {"ch": inner * 2 + core_at})

    def we_arrival(slot, half):
        return remote(we.at[slot, half], we.at[slot, half], we_fwd.at[slot], we_recv.at[slot, half],
                      {"ctx": partner})

    if relay:
        for core_at in range(2):
            @pl.when(jnp.logical_and(is_end, bit_of(core_at) == core))
            def _():
                for slot in range(2):
                    we_copy(slot, core_at).start()

    b_load.start()
    q_load.start()
    for t in range(n_chip):
        w_load(t).start()
        w_copy(t).start()

    def ahead(box, source, r):
        data = box[source, rows_of(r), :]
        spec[source * per + r] = dot(f_ref[0], data) + dot(f_ref[1], data)

    f_load.wait()

    def ahead_own(r, carry):
        ahead(outbox, me, r)
        return carry

    lax.fori_loop(0, per, ahead_own, 0)

    def ahead_others(r, carry):
        for d in range(1, n_ctx):
            source = lax.rem(me + d, n_ctx)
            in_arrival(source, r).wait_recv()
            ahead(inbox, source, r)
        return carry

    lax.fori_loop(0, per, ahead_others, 0)
    b_load.wait()

    rows = 8
    sign = 1.0 - 2.0 * (lax.broadcasted_iota(jnp.int32, (rows, width), 0) % 2).astype(F32)
    done = set()

    def products(m):
        mine = [i * per + m for i in range(n_ctx)]
        need = sorted(set(mine) | {j - 1 for j in mine if j > 0})
        fresh = [j for j in need if j not in done]
        done.update(fresh)
        top_block = max(fresh) + 1

        def one(chunk, carry):
            top = pl.multiple_of(chunk * rows, rows)
            re = pl.ds(top, rows)
            im = pl.ds(pl.multiple_of(BLOCK + top, rows), rows)
            x = [(spec[p, re, :width], spec[p, im, :width]) for p in range(top_block)]
            h = [(spec[p, re, width:], spec[p, im, width:]) for p in range(top_block)]
            z = {}
            for j in fresh:
                zr = zi = None
                for p in range(j + 1):
                    xr, xi = x[p]
                    hr, hi = h[j - p]
                    tr = xr * hr - xi * hi
                    ti = xr * hi + xi * hr
                    zr = tr if zr is None else zr + tr
                    zi = ti if zi is None else zi + ti
                z[j] = (zr, zi)
                zbuf[j, re, :] = zr
                zbuf[j, im, :] = zi

            def get(j):
                return z[j] if j in z else (zbuf[j, re, :], zbuf[j, im, :])

            for i, j in enumerate(mine):
                yr, yi = get(j)
                if j > 0:
                    lr, li = get(j - 1)
                    yr = yr - sign * li
                    yi = yi + sign * lr
                ybuf[i, re, :] = yr
                ybuf[i, im, :] = yi
            return carry

        lax.fori_loop(0, BLOCK // rows, one, 0)

    def back_copy(i, m):
        at = rows_of(m)
        return remote(conv_out.at[i, at], conv_in.at[me, at], back_send.at[i, m], back_recv.at[me, m], {"ctx": i})

    def back_arrival(i, m):
        at = rows_of(m)
        return remote(conv_out.at[i, at], conv_in.at[i, at], back_send.at[i, m], back_recv.at[i, m], {"ctx": i})

    def convolve(m):
        products(m)
        at = rows_of(m)
        for i in range(0, n_ctx, 2):
            data = jnp.concatenate([ybuf[i], ybuf[i + 1]], axis=1)
            high = data.astype(BF16)
            low_part = (data - high.astype(F32)).astype(BF16)
            conv = (dot(b_ref[0], high) + (dot(b_ref[0], low_part) + dot(b_ref[1], high))).astype(BF16)
            for o in range(2):
                part = conv[:, o * width:(o + 1) * width]
                conv_out[i + o, at, :] = part

                @pl.when(me == i + o)
                def _():
                    conv_in[i + o, at, :] = part

                @pl.when(me != i + o)
                def _():
                    back_copy(i + o, m).start()

    def g_copy(m):
        at = rows_of(m)
        return remote(g_ref.at[at], gx.at[at], g_send.at[m], g_recv.at[m], {"ch": mate})

    def gate(m):
        at = rows_of(m)
        for i in range(n_ctx):
            @pl.when(me != i)
            def _():
                back_arrival(i, m).wait_recv()

        for i in range(n_ctx):
            lanes = slice(i * width, (i + 1) * width)
            mixed = outbox[i, at, :width].astype(F32)
            total = conv_in[i, at, :].astype(F32) + skip_ref[:, lanes] * mixed
            g_ref[at, lanes] = (q_ref[at, lanes].astype(F32) * total).astype(BF16)
        g_copy(m).start()

    def share(t, at):
        return dot(g_ref[at, :], w_own[t]) + dot(gx[at, :], wx[t])

    def weights_ready():
        for t in range(n_chip):
            w_load(t).wait()
            w_copy(t).wait()

    if relay:
        n_sub = tokens // SUB
        each = BLOCK // SUB
        to_inner = {"ch": inner * 2 + core}
        to_end = {"ch": end * 2 + core}
        to_across = {"ch": across * 2 + core}

        def sub(s):
            return rows_of(s, SUB)

        def a_from_end(s):
            return remote(send_a.at[sub(s)], recv_a.at[sub(s)], a_send.at[s], a_recv.at[s], to_inner)

        def a_from_mid(s):
            return remote(send_a.at[sub(s)], recv_b.at[sub(s)], a_send.at[s], b_recv.at[s], to_across)

        def b_from_mid(s):
            return remote(send_b.at[sub(s)], recv_b.at[sub(s)], b_send.at[s], b_recv.at[s], to_end)

        def a_arrival(s):
            return remote(send_a.at[sub(s)], recv_a.at[sub(s)], a_send.at[s], a_recv.at[s], to_end)

        def b_arrival(s):
            return remote(send_b.at[sub(s)], recv_b.at[sub(s)], b_send.at[s], b_recv.at[s], to_across)

        def c_copy(s):
            return remote(send_c.at[sub(s)], recv_c.at[sub(s)], c_send.at[s], c_recv.at[s], to_across)

        def ge_copy(s):
            return remote(g_ref.at[sub(s)], ge.at[sub(s)], ge_send.at[s], ge_recv.at[s], to_inner)

        def ge_arrival(s):
            return remote(g_ref.at[sub(s)], ge.at[sub(s)], ge_send.at[s], ge_recv.at[s], to_end)

        def gex_copy(s):
            return remote(ge.at[sub(s)], gex.at[sub(s)], gex_send.at[s], gex_recv.at[s], {"ch": mate})

        def end_step(s, carry):
            part = share(far, sub(s))
            send_a[sub(s), :] = part.astype(BF16)

            @pl.when(s >= 2)
            def _():
                a_from_end(s - 2).wait_send()

            a_from_end(s).start()
            return carry

        def end_first(m):
            @pl.when(is_end)
            def _():
                g_copy(m).wait()
                lax.fori_loop(m * each, (m + 1) * each, end_step, 0)

        def b_step(s):
            part = share(end, sub(s))
            b_arrival(s).wait_recv()
            send_b[sub(s), :] = (part + recv_b[sub(s), :].astype(F32)).astype(BF16)
            b_from_mid(s).start()

        def mid_step(s, carry):
            part = share(far, sub(s))
            a_arrival(s).wait_recv()
            send_a[sub(s), :] = (part + recv_a[sub(s), :].astype(F32)).astype(BF16)
            a_from_mid(s).start()

            @pl.when(s >= 1)
            def _():
                b_step(s - 1)
            return carry

        def mid_first(m):
            @pl.when(is_mid)
            def _():
                g_copy(m).wait()
                lax.fori_loop(m * each, (m + 1) * each, mid_step, 0)

        def pass_weights():
            @pl.when(is_mid)
            def _():
                for slot in range(2):
                    we_arrival(slot, bit).wait_recv()
                    we_arrival(slot, bit).start()

        convolve(0)
        convolve(1)
        q_load.wait()
        gate(0)
        weights_ready()
        end_first(0)
        convolve(2)
        gate(1)
        convolve(3)
        end_first(1)
        pass_weights()
        mid_first(0)
        gate(2)
        end_first(2)
        mid_first(1)
        gate(3)
        end_first(3)
        mid_first(2)
        mid_first(3)

        @pl.when(is_end)
        def _():
            def step(s, carry):
                @pl.when(s < 2)
                def _():
                    a_from_end(n_sub - 2 + s).wait_send()

                @pl.when(s >= 2)
                def _():
                    ge_copy(s - 2).wait_send()

                ge_copy(s).start()
                part = share(chip, sub(s))
                b_arrival(s).wait_recv()
                out_ref[sub(s), :] = (part + recv_b[sub(s), :].astype(F32)).astype(BF16)
                return carry

            lax.fori_loop(0, n_sub, step, 0)
            for s in range(n_sub - 2, n_sub):
                ge_copy(s).wait_send()

        @pl.when(is_mid)
        def _():
            b_step(n_sub - 1)
            for slot in range(2):
                we_arrival(slot, 1 - bit).wait_recv()

            def finish(s):
                c_copy(s).wait_recv()
                out_ref[sub(s), :] = (own[sub(s), :] + recv_c[sub(s), :].astype(F32)).astype(BF16)

            def step(s, carry):
                at = sub(s)
                ge_arrival(s).wait_recv()
                gex_copy(s).start()
                part = share(across, at) + dot(ge[at, :], we[1, core])
                gex_copy(s).wait_recv()
                send_c[at, :] = (part + dot(gex[at, :], we[1, 1 - core])).astype(BF16)
                c_copy(s).start()
                own[at, :] = share(chip, at) + dot(ge[at, :], we[0, core]) + dot(gex[at, :], we[0, 1 - core])

                @pl.when(s >= 1)
                def _():
                    finish(s - 1)
                return carry

            lax.fori_loop(0, n_sub, step, 0)
            finish(n_sub - 1)

            def drain(s, carry):
                a_from_mid(s).wait_send()
                b_from_mid(s).wait_send()
                c_copy(s).wait_send()
                gex_copy(s).wait_send()
                return carry

            lax.fori_loop(0, n_sub, drain, 0)
            for slot in range(2):
                we_arrival(slot, bit).wait_send()

        for core_at in range(2):
            @pl.when(jnp.logical_and(is_end, bit_of(core_at) == core))
            def _():
                for slot in range(2):
                    we_copy(slot, core_at).wait_send()
    else:
        def to_right(t, m):
            at = rows_of(m)
            return remote(send_a.at[t, at], recv_a.at[t, at], a_send.at[t, m], a_recv.at[t, m], {"ch": right})

        def to_left(t, m):
            at = rows_of(m)
            return remote(send_a.at[t, at], recv_b.at[t, at], a_send.at[t, m], b_recv.at[t, m], {"ch": left})

        def arrive_left(t, m):
            at = rows_of(m)
            return remote(send_a.at[t, at], recv_a.at[t, at], a_send.at[t, m], a_recv.at[t, m], {"ch": left})

        def arrive_right(t, m):
            at = rows_of(m)
            return remote(send_a.at[t, at], recv_b.at[t, at], a_send.at[t, m], b_recv.at[t, m], {"ch": right})

        def pass_on(t, m, first, arrived, buffer, copy):
            at = rows_of(m)
            part = share(t, at)

            @pl.when(first)
            def _():
                send_a[t, at, :] = part.astype(BF16)

            @pl.when(jnp.logical_not(first))
            def _():
                arrived(t, m).wait_recv()
                send_a[t, at, :] = (part + buffer[t, at, :].astype(F32)).astype(BF16)

            copy(t, m).start()

        def step(m, carry):
            g_copy(m).wait()
            for d in range(n_chip - 1, 0, -1):
                @pl.when(chip + d < n_chip)
                def _():
                    pass_on(chip + d, m, jnp.logical_not(has_left), arrive_left, recv_a, to_right)

                @pl.when(chip - d >= 0)
                def _():
                    pass_on(chip - d, m, jnp.logical_not(has_right), arrive_right, recv_b, to_left)

            own[rows_of(m), :] = share(chip, rows_of(m))
            return carry

        def finish(m, carry):
            at = rows_of(m)

            @pl.when(has_left)
            def _():
                arrive_left(chip, m).wait_recv()
                own[at, :] += recv_a[chip, at, :].astype(F32)

            @pl.when(has_right)
            def _():
                arrive_right(chip, m).wait_recv()
                own[at, :] += recv_b[chip, at, :].astype(F32)

            out_ref[at, :] = own[at, :].astype(BF16)
            for d in range(n_chip - 1, 0, -1):
                @pl.when(chip + d < n_chip)
                def _():
                    to_right(chip + d, m).wait_send()

                @pl.when(chip - d >= 0)
                def _():
                    to_left(chip - d, m).wait_send()
            return carry

        q_load.wait()
        convolve(0)
        for m in range(1, per):
            convolve(m)
            gate(m - 1)
        gate(per - 1)
        weights_ready()
        lax.fori_loop(0, per, step, 0)
        lax.fori_loop(0, per, finish, 0)

    def drain_ctx(r, carry):
        for i in range(n_ctx):
            @pl.when(me != i)
            def _():
                in_copy(i, r).wait_send()
                back_copy(i, r).wait_send()
        return carry

    lax.fori_loop(0, per, drain_ctx, 0)


def per_device(queries, key_input, value_input, filters, skip_gain, out_weight):
    tokens, channels = queries.shape
    n_ctx = lax.axis_size("ctx")
    n_ch = lax.axis_size("ch")
    n_chip = n_ch // 2
    block = out_weight.shape[1] // n_ch
    width = channels // n_ctx
    per = tokens // BLOCK
    nb = n_ctx * per
    relay = n_chip == 4 and n_ctx == 4 and per == 4
    forward, backward = transform_tables(BLOCK)
    vmem = pl.BlockSpec(memory_space=pltpu.VMEM)
    hbm = pl.BlockSpec(memory_space=pl.ANY)
    dma = pltpu.SemaphoreType.DMA
    n_sub = tokens // SUB
    tiny = (16, 128)
    if relay:
        flows = [(tokens, block)] * 6 + [(tokens, channels)] * 2
        flow_sems = [(n_sub,)] * 10
        we_shape = (2, 2, channels, block)
    else:
        wide = (n_chip, tokens, block)
        flows = [wide, tiny, tiny, wide, wide, tiny, tiny, tiny]
        flow_sems = [(n_chip, per)] * 10
        we_shape = (2, 2, 16, 128)
    return pl.pallas_call(
        functools.partial(layer_kernel, n_ctx, n_ch, relay),
        out_shape=jax.ShapeDtypeStruct((tokens, block), BF16),
        in_specs=[hbm] * 4 + [vmem] + [hbm] * 3,
        out_specs=vmem,
        scratch_shapes=[
            pltpu.VMEM((tokens, channels), BF16),
            pltpu.VMEM((tokens, channels), BF16),
            pltpu.VMEM((tokens, channels), BF16),
            pltpu.VMEM((tokens, channels), BF16),
            pltpu.VMEM(forward.shape, BF16),
            pltpu.VMEM(backward.shape, BF16),
            pltpu.VMEM((n_chip, channels, block), BF16),
            pltpu.VMEM((n_chip, channels, block), BF16),
            pltpu.VMEM(we_shape, BF16),
            pltpu.VMEM((n_ctx, tokens, 2 * width), BF16),
            pltpu.VMEM((n_ctx, tokens, 2 * width), BF16),
            pltpu.VMEM((nb, 2 * BLOCK, 2 * width), F32),
            pltpu.VMEM((nb, 2 * BLOCK, width), F32),
            pltpu.VMEM((n_ctx, 2 * BLOCK, width), F32),
            pltpu.VMEM((n_ctx, tokens, width), BF16),
            pltpu.VMEM((n_ctx, tokens, width), BF16),
            pltpu.VMEM((tokens, channels), BF16),
            pltpu.VMEM((tokens, channels), BF16),
        ] + [pltpu.VMEM(shape, BF16) for shape in flows] + [
            pltpu.VMEM((tokens, block), F32),
            dma((3, per)), dma((3,)), dma((n_chip,)), dma((n_chip,)), dma((n_chip,)),
            dma((2, 2)), dma((2, 2)), dma((2,)),
            dma((n_ctx, per)), dma((n_ctx, per)), dma((n_ctx, per)), dma((n_ctx, per)),
            dma((per,)), dma((per,)),
        ] + [dma(shape) for shape in flow_sems],
        compiler_params=pltpu.CompilerParams(
            collective_id=0, has_side_effects=True, vmem_limit_bytes=60 * 1024 * 1024
        ),
        cost_estimate=pl.CostEstimate(
            flops=28 * n_ctx * tokens * BLOCK * width + 2 * tokens * channels * n_ch * block,
            bytes_accessed=12 * tokens * channels + 2 * channels * n_ch * block, transcendentals=0,
        ),
    )(queries, key_input, value_input, filters, skip_gain[None, :],
      jnp.asarray(forward), jnp.asarray(backward), out_weight)


def solution(mesh):
    in_specs = (
        P("ctx", "ch"),
        P("ctx", "ch"),
        P("ctx", "ch"),
        P("ctx", "ch"),
        P("ch"),
        P("ch", None),
    )
    return jax.shard_map(
        per_device, mesh=mesh, in_specs=in_specs, out_specs=P("ctx", "ch"), check_vma=False
    )
```

time: 133 us -> 101 us (0.76)
  Pallas kernels: 128 us -> 98.2 us
  local copies, waits for them, and re-layouts: 3.78 us -> 2.26 us
    pallas_call x2 -> x1, Pallas kernels: 128 us -> 98.2 us  [per_device(): pl.pallas_call(functools.partial(layer_kernel, n_ctx, n_ch, relay), out_s...]
    unnamed x5 -> x1, local copies, waits for them, and re-layouts: 3.78 us -> 2.26 us
where the time goes in v1:
time: 101 us; the launch traced here: 100 us
  Pallas kernels  98.2 us (97%)
  local copies, waits for them, and re-layouts  2.26 us (2%)
    pallas_call x1, Pallas kernels, per_device(): pl.pallas_call(functools.partial(layer_kernel, n_ctx, n_ch, relay), out_s...  98.2 us
    unnamed x1, local copies, waits for them, and re-layouts  2.26 us

profile of v1, /device:TPU:10, one launch (start us, length us, event | category | flops | bytes accessed | tf_op | source)
XLA Modules:
  0.0 100.5 jit_solution(4989886245490360080)
XLA Ops:
  0.0 98.2 %shard_map.82 = bf16[1024,512]{1,0:T(8,128)(2,1)} custom-call(bf16[1024,512]{1,0:T(8,128)(2,1)} %q_hbm.1, bf16[1024,512]{1,0:T(8,128)(2,1)} %k_hbm.1, bf16[1024,512]{1,0:T(8,128)(2,1)} %v_hbm.1, bf16[1024,512]{1,0:T(8,128)(2,1)} %h_hbm.1, f32[1,512]{1,0:T(1,128)} %bitcast.1, bf16[2,512,256]{2,1,0:T(8,128)(2,1)} %constant.4.clone.f_hbm, ...), custom_call_target="tpu_custom_call" | custom-call | flops 8053063680 | bytes 10485760 | tf_op jit(solution)/shard_map/pallas_call | solution.py:585
  98.2 2.3 %copy.10 = bf16[1024,512]{1,0:T(8,128)(2,1)} copy(bf16[1024,512]{1,0:T(8,128)(2,1)} %shard_map.82) | data formatting | bytes 2097152

commit v2 on v1

--- a/solution.py
+++ b/solution.py
@@ -9,7 +9,11 @@
 from jax.sharding import PartitionSpec as P
 
 BLOCK = 256
-SUB = 128
+PIECE = 128
+SUB = 64
+WINDOW = 4
+B_LAG = 4
+VMEM_MIB = 56
 F32 = jnp.float32
 BF16 = jnp.bfloat16
 
@@ -40,7 +44,7 @@
 
 def layer_kernel(n_ctx, n_ch, relay, q_hbm, k_hbm, v_hbm, h_hbm, skip_ref, f_hbm, b_hbm, w_hbm, out_ref,
                  q_ref, k_ref, v_ref, h_ref, f_ref, b_ref, w_own, wx, we,
-                 outbox, inbox, spec, zbuf, ybuf, conv_out, conv_in, g_ref, gx,
+                 outbox, inbox, spec, zbuf, ybuf, yhigh, ylow, conv_out, conv_in, g_ref, gx,
                  send_a, send_b, send_c, recv_a, recv_b, recv_c, ge, gex, own,
                  load_sem, table_sem, w_sem, w_send, w_recv, we_send, we_recv, we_fwd,
                  in_send, in_recv, back_send, back_recv, g_send, g_recv,
@@ -54,6 +58,7 @@
     tokens, block = out_ref.shape
     width = conv_in.shape[2]
     per = tokens // BLOCK
+    halves = BLOCK // PIECE
     has_left = chip > 0
     has_right = chip < n_chip - 1
     left = jnp.maximum(ch - 2, core)
@@ -194,11 +199,51 @@
             ahead(inbox, source, r)
         return carry
 
-    lax.fori_loop(0, per, ahead_others, 0)
-    b_load.wait()
-
+    nb = n_ctx * per
     rows = 8
     sign = 1.0 - 2.0 * (lax.broadcasted_iota(jnp.int32, (rows, width), 0) % 2).astype(F32)
+
+    def parts_of(chunk):
+        top = pl.multiple_of(chunk * rows, rows)
+        return pl.ds(top, rows), pl.ds(pl.multiple_of(BLOCK + top, rows), rows)
+
+    def is_last(p):
+        return p % per == per - 1
+
+    def sums(blocks, late, start, re, im):
+        pairs = {j: [p for p in range(j + 1) if (is_last(p) or is_last(j - p)) == late] for j in blocks}
+        used = {p for j in blocks for p in pairs[j]} | {j - p for j in blocks for p in pairs[j]}
+        x = {p: (spec[p, re, :width], spec[p, im, :width]) for p in used}
+        h = {p: (spec[p, re, width:], spec[p, im, width:]) for p in used}
+        z = {}
+        for j in blocks:
+            zr, zi = start[j] if j in start else (None, None)
+            for p in pairs[j]:
+                xr, xi = x[p]
+                hr, hi = h[j - p]
+                tr = xr * hr - xi * hi
+                ti = xr * hi + xi * hr
+                zr = tr if zr is None else zr + tr
+                zi = ti if zi is None else zi + ti
+            z[j] = (zr, zi)
+        return z
+
+    def has_early(j):
+        return any(not is_last(p) and not is_last(j - p) for p in range(j + 1))
+
+    early = [j for j in range(nb) if has_early(j)]
+
+    def early_sums(chunk, carry):
+        re, im = parts_of(chunk)
+        for j, (zr, zi) in sums(early, False, {}, re, im).items():
+            zbuf[j, re, :] = zr
+            zbuf[j, im, :] = zi
+        return carry
+
+    lax.fori_loop(0, per - 1, ahead_others, 0)
+    lax.fori_loop(0, BLOCK // rows, early_sums, 0)
+    ahead_others(per - 1, 0)
+    b_load.wait()
     done = set()
 
     def products(m):
@@ -206,27 +251,14 @@
         need = sorted(set(mine) | {j - 1 for j in mine if j > 0})
         fresh = [j for j in need if j not in done]
         done.update(fresh)
-        top_block = max(fresh) + 1
 
         def one(chunk, carry):
-            top = pl.multiple_of(chunk * rows, rows)
-            re = pl.ds(top, rows)
-            im = pl.ds(pl.multiple_of(BLOCK + top, rows), rows)
-            x = [(spec[p, re, :width], spec[p, im, :width]) for p in range(top_block)]
-            h = [(spec[p, re, width:], spec[p, im, width:]) for p in range(top_block)]
-            z = {}
+            re, im = parts_of(chunk)
+            start = {j: (zbuf[j, re, :], zbuf[j, im, :]) for j in fresh if j in early}
+            z = sums(fresh, True, start, re, im)
             for j in fresh:
-                zr = zi = None
-                for p in range(j + 1):
-                    xr, xi = x[p]
-                    hr, hi = h[j - p]
-                    tr = xr * hr - xi * hi
-                    ti = xr * hi + xi * hr
-                    zr = tr if zr is None else zr + tr
-                    zi = ti if zi is None else zi + ti
-                z[j] = (zr, zi)
-                zbuf[j, re, :] = zr
-                zbuf[j, im, :] = zi
+                zbuf[j, re, :] = z[j][0]
+                zbuf[j, im, :] = z[j][1]
 
             def get(j):
                 return z[j] if j in z else (zbuf[j, re, :], zbuf[j, im, :])
@@ -242,23 +274,31 @@
             return carry
 
         lax.fori_loop(0, BLOCK // rows, one, 0)
-
-    def back_copy(i, m):
-        at = rows_of(m)
-        return remote(conv_out.at[i, at], conv_in.at[me, at], back_send.at[i, m], back_recv.at[me, m], {"ctx": i})
-
-    def back_arrival(i, m):
-        at = rows_of(m)
-        return remote(conv_out.at[i, at], conv_in.at[i, at], back_send.at[i, m], back_recv.at[i, m], {"ctx": i})
-
-    def convolve(m):
-        products(m)
-        at = rows_of(m)
         for i in range(0, n_ctx, 2):
             data = jnp.concatenate([ybuf[i], ybuf[i + 1]], axis=1)
             high = data.astype(BF16)
-            low_part = (data - high.astype(F32)).astype(BF16)
-            conv = (dot(b_ref[0], high) + (dot(b_ref[0], low_part) + dot(b_ref[1], high))).astype(BF16)
+            yhigh[i // 2] = high
+            ylow[i // 2] = (data - high.astype(F32)).astype(BF16)
+
+    def piece(m):
+        return rows_of(m, PIECE)
+
+    def back_copy(i, m):
+        at = piece(m)
+        return remote(conv_out.at[i, at], conv_in.at[me, at], back_send.at[i, m], back_recv.at[me, m], {"ctx": i})
+
+    def back_arrival(i, m):
+        at = piece(m)
+        return remote(conv_out.at[i, at], conv_in.at[i, at], back_send.at[i, m], back_recv.at[i, m], {"ctx": i})
+
+    def inverse(m):
+        at = piece(m)
+        inside = slice((m % halves) * PIECE, (m % halves + 1) * PIECE)
+        b_high = b_ref[0, inside, :]
+        b_low = b_ref[1, inside, :]
+        for i in range(0, n_ctx, 2):
+            high = yhigh[i // 2]
+            conv = (dot(b_high, high) + (dot(b_high, ylow[i // 2]) + dot(b_low, high))).astype(BF16)
             for o in range(2):
                 part = conv[:, o * width:(o + 1) * width]
                 conv_out[i + o, at, :] = part
@@ -272,11 +312,11 @@
                     back_copy(i + o, m).start()
 
     def g_copy(m):
-        at = rows_of(m)
+        at = piece(m)
         return remote(g_ref.at[at], gx.at[at], g_send.at[m], g_recv.at[m], {"ch": mate})
 
     def gate(m):
-        at = rows_of(m)
+        at = piece(m)
         for i in range(n_ctx):
             @pl.when(me != i)
             def _():
@@ -299,7 +339,8 @@
 
     if relay:
         n_sub = tokens // SUB
-        each = BLOCK // SUB
+        each = PIECE // SUB
+        n_piece = tokens // PIECE
         to_inner = {"ch": inner * 2 + core}
         to_end = {"ch": end * 2 + core}
         to_across = {"ch": across * 2 + core}
@@ -334,45 +375,38 @@
         def gex_copy(s):
             return remote(ge.at[sub(s)], gex.at[sub(s)], gex_send.at[s], gex_recv.at[s], {"ch": mate})
 
-        def end_step(s, carry):
-            part = share(far, sub(s))
-            send_a[sub(s), :] = part.astype(BF16)
-
-            @pl.when(s >= 2)
-            def _():
-                a_from_end(s - 2).wait_send()
-
-            a_from_end(s).start()
-            return carry
-
         def end_first(m):
             @pl.when(is_end)
             def _():
                 g_copy(m).wait()
-                lax.fori_loop(m * each, (m + 1) * each, end_step, 0)
+                part = share(far, piece(m))
+                for o in range(each):
+                    s = m * each + o
+                    send_a[sub(s), :] = part[o * SUB:(o + 1) * SUB].astype(BF16)
+                    if s >= WINDOW:
+                        a_from_end(s - WINDOW).wait_send()
+                    a_from_end(s).start()
 
         def b_step(s):
-            part = share(end, sub(s))
             b_arrival(s).wait_recv()
-            send_b[sub(s), :] = (part + recv_b[sub(s), :].astype(F32)).astype(BF16)
+            send_b[sub(s), :] = (own[sub(s), :] + recv_b[sub(s), :].astype(F32)).astype(BF16)
             b_from_mid(s).start()
-
-        def mid_step(s, carry):
-            part = share(far, sub(s))
-            a_arrival(s).wait_recv()
-            send_a[sub(s), :] = (part + recv_a[sub(s), :].astype(F32)).astype(BF16)
-            a_from_mid(s).start()
-
-            @pl.when(s >= 1)
-            def _():
-                b_step(s - 1)
-            return carry
 
         def mid_first(m):
             @pl.when(is_mid)
             def _():
                 g_copy(m).wait()
-                lax.fori_loop(m * each, (m + 1) * each, mid_step, 0)
+                own[piece(m), :] = share(end, piece(m))
+                part = share(far, piece(m))
+                for o in range(each):
+                    s = m * each + o
+                    a_arrival(s).wait_recv()
+                    send_a[sub(s), :] = (
+                        part[o * SUB:(o + 1) * SUB] + recv_a[sub(s), :].astype(F32)
+                    ).astype(BF16)
+                    a_from_mid(s).start()
+                    if s >= B_LAG:
+                        b_step(s - B_LAG)
 
         def pass_weights():
             @pl.when(is_mid)
@@ -381,74 +415,98 @@
                     we_arrival(slot, bit).wait_recv()
                     we_arrival(slot, bit).start()
 
-        convolve(0)
-        convolve(1)
+        products(0)
+        inverse(0)
+        inverse(1)
+        products(1)
         q_load.wait()
         gate(0)
         weights_ready()
+        inverse(2)
         end_first(0)
-        convolve(2)
         gate(1)
-        convolve(3)
+        inverse(3)
         end_first(1)
+        products(2)
+        gate(2)
+        inverse(4)
+        end_first(2)
+        mid_first(0)
+        gate(3)
+        inverse(5)
+        end_first(3)
+        mid_first(1)
+        products(3)
+        inverse(6)
+        inverse(7)
         pass_weights()
-        mid_first(0)
-        gate(2)
-        end_first(2)
-        mid_first(1)
-        gate(3)
-        end_first(3)
-        mid_first(2)
-        mid_first(3)
+        for m in range(4, 8):
+            gate(m)
+            end_first(m)
+            mid_first(m - 2)
+        mid_first(6)
+        mid_first(7)
 
         @pl.when(is_end)
         def _():
-            def step(s, carry):
-                @pl.when(s < 2)
-                def _():
-                    a_from_end(n_sub - 2 + s).wait_send()
-
-                @pl.when(s >= 2)
-                def _():
-                    ge_copy(s - 2).wait_send()
-
-                ge_copy(s).start()
-                part = share(chip, sub(s))
-                b_arrival(s).wait_recv()
-                out_ref[sub(s), :] = (part + recv_b[sub(s), :].astype(F32)).astype(BF16)
+            for s in range(n_sub - WINDOW, n_sub):
+                a_from_end(s).wait_send()
+
+            def step(p, carry):
+                for o in range(each):
+                    s = p * each + o
+
+                    @pl.when(s >= WINDOW)
+                    def _():
+                        ge_copy(s - WINDOW).wait_send()
+
+                    ge_copy(s).start()
+                at = piece(p)
+                part = share(chip, at)
+                for o in range(each):
+                    b_arrival(p * each + o).wait_recv()
+                out_ref[at, :] = (part + recv_b[at, :].astype(F32)).astype(BF16)
                 return carry
 
-            lax.fori_loop(0, n_sub, step, 0)
-            for s in range(n_sub - 2, n_sub):
+            lax.fori_loop(0, n_piece, step, 0)
+            for s in range(n_sub - WINDOW, n_sub):
                 ge_copy(s).wait_send()
 
         @pl.when(is_mid)
         def _():
-            b_step(n_sub - 1)
+            for s in range(n_sub - B_LAG, n_sub):
+                b_step(s)
             for slot in range(2):
                 we_arrival(slot, 1 - bit).wait_recv()
 
-            def finish(s):
-                c_copy(s).wait_recv()
-                out_ref[sub(s), :] = (own[sub(s), :] + recv_c[sub(s), :].astype(F32)).astype(BF16)
-
-            def step(s, carry):
-                at = sub(s)
-                ge_arrival(s).wait_recv()
-                gex_copy(s).start()
+            def finish(p):
+                at = piece(p)
+                for o in range(each):
+                    c_copy(p * each + o).wait_recv()
+                out_ref[at, :] = (own[at, :] + recv_c[at, :].astype(F32)).astype(BF16)
+
+            def step(p, carry):
+                at = piece(p)
+                for o in range(each):
+                    ge_arrival(p * each + o).wait_recv()
+                    gex_copy(p * each + o).start()
                 part = share(across, at) + dot(ge[at, :], we[1, core])
-                gex_copy(s).wait_recv()
+                own[at, :] = share(chip, at) + dot(ge[at, :], we[0, core])
+                for o in range(each):
+                    gex_copy(p * each + o).wait_recv()
                 send_c[at, :] = (part + dot(gex[at, :], we[1, 1 - core])).astype(BF16)
-                c_copy(s).start()
-                own[at, :] = share(chip, at) + dot(ge[at, :], we[0, core]) + dot(gex[at, :], we[0, 1 - core])
-
-                @pl.when(s >= 1)
+                for o in range(each):
+                    c_copy(p * each + o).start()
+                own[at, :] += dot(gex[at, :], we[0, 1 - core])
+
+                @pl.when(p >= 2)
                 def _():
-                    finish(s - 1)
+                    finish(p - 2)
                 return carry
 
-            lax.fori_loop(0, n_sub, step, 0)
-            finish(n_sub - 1)
+            lax.fori_loop(0, n_piece, step, 0)
+            for p in range(n_piece - 2, n_piece):
+                finish(p)
 
             def drain(s, carry):
                 a_from_mid(s).wait_send()
@@ -499,7 +557,8 @@
             copy(t, m).start()
 
         def step(m, carry):
-            g_copy(m).wait()
+            for o in range(halves):
+                g_copy(m * halves + o).wait()
             for d in range(n_chip - 1, 0, -1):
                 @pl.when(chip + d < n_chip)
                 def _():
@@ -537,11 +596,15 @@
             return carry
 
         q_load.wait()
-        convolve(0)
-        for m in range(1, per):
-            convolve(m)
-            gate(m - 1)
-        gate(per - 1)
+        for m in range(per):
+            products(m)
+            for o in range(halves):
+                inverse(m * halves + o)
+            if m > 0:
+                for o in range(halves):
+                    gate((m - 1) * halves + o)
+        for o in range(halves):
+            gate((per - 1) * halves + o)
         weights_ready()
         lax.fori_loop(0, per, step, 0)
         lax.fori_loop(0, per, finish, 0)
@@ -551,7 +614,8 @@
             @pl.when(me != i)
             def _():
                 in_copy(i, r).wait_send()
-                back_copy(i, r).wait_send()
+                for o in range(halves):
+                    back_copy(i, r * halves + o).wait_send()
         return carry
 
     lax.fori_loop(0, per, drain_ctx, 0)
@@ -572,6 +636,7 @@
     hbm = pl.BlockSpec(memory_space=pl.ANY)
     dma = pltpu.SemaphoreType.DMA
     n_sub = tokens // SUB
+    pieces = tokens // PIECE
     tiny = (16, 128)
     if relay:
         flows = [(tokens, block)] * 6 + [(tokens, channels)] * 2
@@ -602,6 +667,8 @@
             pltpu.VMEM((nb, 2 * BLOCK, 2 * width), F32),
             pltpu.VMEM((nb, 2 * BLOCK, width), F32),
             pltpu.VMEM((n_ctx, 2 * BLOCK, width), F32),
+            pltpu.VMEM((n_ctx // 2, 2 * BLOCK, 2 * width), BF16),
+            pltpu.VMEM((n_ctx // 2, 2 * BLOCK, 2 * width), BF16),
             pltpu.VMEM((n_ctx, tokens, width), BF16),
             pltpu.VMEM((n_ctx, tokens, width), BF16),
             pltpu.VMEM((tokens, channels), BF16),
@@ -610,11 +677,11 @@
             pltpu.VMEM((tokens, block), F32),
             dma((3, per)), dma((3,)), dma((n_chip,)), dma((n_chip,)), dma((n_chip,)),
             dma((2, 2)), dma((2, 2)), dma((2,)),
-            dma((n_ctx, per)), dma((n_ctx, per)), dma((n_ctx, per)), dma((n_ctx, per)),
-            dma((per,)), dma((per,)),
+            dma((n_ctx, per)), dma((n_ctx, per)), dma((n_ctx, pieces)), dma((n_ctx, pieces)),
+            dma((pieces,)), dma((pieces,)),
         ] + [dma(shape) for shape in flow_sems],
         compiler_params=pltpu.CompilerParams(
-            collective_id=0, has_side_effects=True, vmem_limit_bytes=60 * 1024 * 1024
+            collective_id=0, has_side_effects=True, vmem_limit_bytes=VMEM_MIB * 1024 * 1024
         ),
         cost_estimate=pl.CostEstimate(
             flops=28 * n_ctx * tokens * BLOCK * width + 2 * tokens * channels * n_ch * block,

time: 101 us -> 97.2 us (0.962)
  Pallas kernels: 98.2 us -> 93.8 us
    pallas_call x1, Pallas kernels: 98.2 us -> 93.8 us  [per_device(): pl.pallas_call(functools.partial(layer_kernel, n_ctx, n_ch, relay), out_s...]
where the time goes in v2:
time: 97.2 us; the launch traced here: 96.1 us
  Pallas kernels  93.8 us (97%)
  local copies, waits for them, and re-layouts  2.26 us (2%)
    pallas_call x1, Pallas kernels, per_device(): pl.pallas_call(functools.partial(layer_kernel, n_ctx, n_ch, relay), out_s...  93.8 us
    unnamed x1, local copies, waits for them, and re-layouts  2.26 us

profile of v2, /device:TPU:10, one launch (start us, length us, event | category | flops | bytes accessed | tf_op | source)
XLA Modules:
  0.0 96.1 jit_solution(12796604036714619995)
XLA Ops:
  0.0 93.8 %shard_map.82 = bf16[1024,512]{1,0:T(8,128)(2,1)} custom-call(bf16[1024,512]{1,0:T(8,128)(2,1)} %q_hbm.1, bf16[1024,512]{1,0:T(8,128)(2,1)} %k_hbm.1, bf16[1024,512]{1,0:T(8,128)(2,1)} %v_hbm.1, bf16[1024,512]{1,0:T(8,128)(2,1)} %h_hbm.1, f32[1,512]{1,0:T(1,128)} %bitcast.1, bf16[2,512,256]{2,1,0:T(8,128)(2,1)} %constant.4.clone.f_hbm, ...), custom_call_target="tpu_custom_call" | custom-call | flops 8053063680 | bytes 10485760 | tf_op jit(solution)/shard_map/pallas_call | solution.py:650
  93.8 2.3 %copy.10 = bf16[1024,512]{1,0:T(8,128)(2,1)} copy(bf16[1024,512]{1,0:T(8,128)(2,1)} %shard_map.82) | data formatting | bytes 2097152

commit v3 on v2

--- a/solution.py
+++ b/solution.py
@@ -12,6 +12,8 @@
 PIECE = 128
 SUB = 64
 WINDOW = 4
+FINE = 1
+AHEAD = 1
 B_LAG = 4
 VMEM_MIB = 56
 F32 = jnp.float32
@@ -42,8 +44,8 @@
 MESH = pl.DeviceIdType.MESH
 
 
-def layer_kernel(n_ctx, n_ch, relay, q_hbm, k_hbm, v_hbm, h_hbm, skip_ref, f_hbm, b_hbm, w_hbm, out_ref,
-                 q_ref, k_ref, v_ref, h_ref, f_ref, b_ref, w_own, wx, we,
+def layer_kernel(n_ctx, n_ch, relay, q_hbm, k_hbm, v_hbm, h_hbm, skip_ref, f_hbm, b_hbm, w_hbm, out_hbm,
+                 out_ref, out_sem, q_ref, k_ref, v_ref, h_ref, f_ref, b_ref, w_own, wx, we,
                  outbox, inbox, spec, zbuf, ybuf, yhigh, ylow, conv_out, conv_in, g_ref, gx,
                  send_a, send_b, send_c, recv_a, recv_b, recv_c, ge, gex, own,
                  load_sem, table_sem, w_sem, w_send, w_recv, we_send, we_recv, we_fwd,
@@ -311,6 +313,10 @@
                 def _():
                     back_copy(i + o, m).start()
 
+    def out_copy(m):
+        at = piece(m)
+        return pltpu.make_async_copy(out_ref.at[at], out_hbm.at[at], out_sem.at[m])
+
     def g_copy(m):
         at = piece(m)
         return remote(g_ref.at[at], gx.at[at], g_send.at[m], g_recv.at[m], {"ch": mate})
@@ -421,6 +427,12 @@
         products(1)
         q_load.wait()
         gate(0)
+
+        @pl.when(is_end)
+        def _():
+            for s in range(AHEAD):
+                ge_copy(s).start()
+
         weights_ready()
         inverse(2)
         end_first(0)
@@ -460,12 +472,16 @@
                     def _():
                         ge_copy(s - WINDOW).wait_send()
 
-                    ge_copy(s).start()
+                    @pl.when(s >= AHEAD)
+                    def _():
+                        ge_copy(s).start()
+
                 at = piece(p)
                 part = share(chip, at)
                 for o in range(each):
                     b_arrival(p * each + o).wait_recv()
                 out_ref[at, :] = (part + recv_b[at, :].astype(F32)).astype(BF16)
+                out_copy(p).start()
                 return carry
 
             lax.fori_loop(0, n_piece, step, 0)
@@ -474,8 +490,6 @@
 
         @pl.when(is_mid)
         def _():
-            for s in range(n_sub - B_LAG, n_sub):
-                b_step(s)
             for slot in range(2):
                 we_arrival(slot, 1 - bit).wait_recv()
 
@@ -484,28 +498,49 @@
                 for o in range(each):
                     c_copy(p * each + o).wait_recv()
                 out_ref[at, :] = (own[at, :] + recv_c[at, :].astype(F32)).astype(BF16)
+                out_copy(p).start()
+
+            def relay_rows(at, subs):
+                part = share(across, at)
+                own_part = share(chip, at)
+                for s in subs:
+                    ge_arrival(s).wait_recv()
+                    gex_copy(s).start()
+                part += dot(ge[at, :], we[1, core])
+                own_part += dot(ge[at, :], we[0, core])
+                for s in subs:
+                    gex_copy(s).wait_recv()
+                send_c[at, :] = (part + dot(gex[at, :], we[1, 1 - core])).astype(BF16)
+                for s in subs:
+                    c_copy(s).start()
+                own[at, :] = own_part + dot(gex[at, :], we[0, 1 - core])
 
             def step(p, carry):
-                at = piece(p)
-                for o in range(each):
-                    ge_arrival(p * each + o).wait_recv()
-                    gex_copy(p * each + o).start()
-                part = share(across, at) + dot(ge[at, :], we[1, core])
-                own[at, :] = share(chip, at) + dot(ge[at, :], we[0, core])
-                for o in range(each):
-                    gex_copy(p * each + o).wait_recv()
-                send_c[at, :] = (part + dot(gex[at, :], we[1, 1 - core])).astype(BF16)
-                for o in range(each):
-                    c_copy(p * each + o).start()
-                own[at, :] += dot(gex[at, :], we[0, 1 - core])
+                relay_rows(piece(p), [p * each + o for o in range(each)])
 
                 @pl.when(p >= 2)
                 def _():
                     finish(p - 2)
                 return carry
 
-            lax.fori_loop(0, n_piece, step, 0)
-            for p in range(n_piece - 2, n_piece):
+            late = list(range(n_sub - B_LAG, n_sub))
+            for s in range(each):
+                relay_rows(sub(s), [s])
+                if s > 0:
+                    b_step(late.pop(0))
+            for p in range(1, 3):
+                relay_rows(piece(p), [p * each + o for o in range(each)])
+                for s in late[:2]:
+                    b_step(s)
+                late = late[2:]
+            for s in late:
+                b_step(s)
+            finish(0)
+            lax.fori_loop(3, n_piece - FINE, step, 0)
+            finish(n_piece - FINE - 2)
+            for s in range((n_piece - FINE) * each, n_sub):
+                relay_rows(sub(s), [s])
+            for p in range(n_piece - FINE - 1, n_piece):
                 finish(p)
 
             def drain(s, carry):
@@ -585,6 +620,8 @@
                 own[at, :] += recv_b[chip, at, :].astype(F32)
 
             out_ref[at, :] = own[at, :].astype(BF16)
+            for o in range(halves):
+                out_copy(m * halves + o).start()
             for d in range(n_chip - 1, 0, -1):
                 @pl.when(chip + d < n_chip)
                 def _():
@@ -619,6 +656,12 @@
         return carry
 
     lax.fori_loop(0, per, drain_ctx, 0)
+
+    def drain_out(m, carry):
+        out_copy(m).wait()
+        return carry
+
+    lax.fori_loop(0, tokens // PIECE, drain_out, 0)
 
 
 def per_device(queries, key_input, value_input, filters, skip_gain, out_weight):
@@ -651,8 +694,10 @@
         functools.partial(layer_kernel, n_ctx, n_ch, relay),
         out_shape=jax.ShapeDtypeStruct((tokens, block), BF16),
         in_specs=[hbm] * 4 + [vmem] + [hbm] * 3,
-        out_specs=vmem,
+        out_specs=hbm,
         scratch_shapes=[
+            pltpu.VMEM((tokens, block), BF16),
+            dma((pieces,)),
             pltpu.VMEM((tokens, channels), BF16),
             pltpu.VMEM((tokens, channels), BF16),
             pltpu.VMEM((tokens, channels), BF16),

time: 97.2 us -> 95 us (0.977)
  Pallas kernels: 93.8 us -> 91.7 us
    pallas_call x1, Pallas kernels: 93.8 us -> 91.7 us  [per_device(): pl.pallas_call(functools.partial(layer_kernel, n_ctx, n_ch, relay), out_s...]
where the time goes in v3:
time: 95 us; the launch traced here: 94 us
  Pallas kernels  91.7 us (97%)
  local copies, waits for them, and re-layouts  2.26 us (2%)
    pallas_call x1, Pallas kernels, per_device(): pl.pallas_call(functools.partial(layer_kernel, n_ctx, n_ch, relay), out_s...  91.7 us
    unnamed x1, local copies, waits for them, and re-layouts  2.26 us

profile of v3, /device:TPU:10, one launch (start us, length us, event | category | flops | bytes accessed | tf_op | source)
XLA Modules:
  0.0 94.0 jit_solution(18353206679802572633)
XLA Ops:
  0.0 91.7 %shard_map.82 = bf16[1024,512]{1,0:T(8,128)(2,1)} custom-call(bf16[1024,512]{1,0:T(8,128)(2,1)} %q_hbm.1, bf16[1024,512]{1,0:T(8,128)(2,1)} %k_hbm.1, bf16[1024,512]{1,0:T(8,128)(2,1)} %v_hbm.1, bf16[1024,512]{1,0:T(8,128)(2,1)} %h_hbm.1, f32[1,512]{1,0:T(1,128)} %bitcast.1, bf16[2,512,256]{2,1,0:T(8,128)(2,1)} %constant.4.clone.f_hbm, ...), custom_call_target="tpu_custom_call" | custom-call | flops 8053063680 | bytes 10485760 | tf_op jit(solution)/shard_map/pallas_call | solution.py:693
  91.7 2.3 %copy.10 = bf16[1024,512]{1,0:T(8,128)(2,1)} copy(bf16[1024,512]{1,0:T(8,128)(2,1)} %shard_map.82) | data formatting | bytes 2097152

commit v4 on v3

--- a/solution.py
+++ b/solution.py
@@ -12,8 +12,7 @@
 PIECE = 128
 SUB = 64
 WINDOW = 4
-FINE = 1
-AHEAD = 1
+AHEAD = 2
 B_LAG = 4
 VMEM_MIB = 56
 F32 = jnp.float32
@@ -47,7 +46,7 @@
 def layer_kernel(n_ctx, n_ch, relay, q_hbm, k_hbm, v_hbm, h_hbm, skip_ref, f_hbm, b_hbm, w_hbm, out_hbm,
                  out_ref, out_sem, q_ref, k_ref, v_ref, h_ref, f_ref, b_ref, w_own, wx, we,
                  outbox, inbox, spec, zbuf, ybuf, yhigh, ylow, conv_out, conv_in, g_ref, gx,
-                 send_a, send_b, send_c, recv_a, recv_b, recv_c, ge, gex, own,
+                 send_a, send_b, send_c, recv_a, recv_b, recv_c, ge, gex, own, ahead_c,
                  load_sem, table_sem, w_sem, w_send, w_recv, we_send, we_recv, we_fwd,
                  in_send, in_recv, back_send, back_recv, g_send, g_recv,
                  a_send, a_recv, b_send, b_recv, c_send, c_recv, ge_send, ge_recv, gex_send, gex_recv):
@@ -457,6 +456,16 @@
             end_first(m)
             mid_first(m - 2)
         mid_first(6)
+
+        def own_shares(p):
+            at = piece(p)
+            ahead_c[at, :] = share(across, at)
+            own[at, :] = share(chip, at)
+
+        @pl.when(is_mid)
+        def _():
+            own_shares(0)
+
         mid_first(7)
 
         @pl.when(is_end)
@@ -500,47 +509,51 @@
                 out_ref[at, :] = (own[at, :] + recv_c[at, :].astype(F32)).astype(BF16)
                 out_copy(p).start()
 
-            def relay_rows(at, subs):
-                part = share(across, at)
-                own_part = share(chip, at)
+            def relay_rows(at, subs, between):
                 for s in subs:
                     ge_arrival(s).wait_recv()
                     gex_copy(s).start()
-                part += dot(ge[at, :], we[1, core])
-                own_part += dot(ge[at, :], we[0, core])
+                part = ahead_c[at, :] + dot(ge[at, :], we[1, core])
+                own[at, :] += dot(ge[at, :], we[0, core])
+                between()
                 for s in subs:
                     gex_copy(s).wait_recv()
                 send_c[at, :] = (part + dot(gex[at, :], we[1, 1 - core])).astype(BF16)
                 for s in subs:
                     c_copy(s).start()
-                own[at, :] = own_part + dot(gex[at, :], we[0, 1 - core])
-
-            def step(p, carry):
-                relay_rows(piece(p), [p * each + o for o in range(each)])
-
-                @pl.when(p >= 2)
-                def _():
-                    finish(p - 2)
-                return carry
+                own[at, :] += dot(gex[at, :], we[0, 1 - core])
+
+            def relay_piece(p, between):
+                relay_rows(piece(p), [p * each + o for o in range(each)], between)
+
+            def nothing():
+                pass
 
             late = list(range(n_sub - B_LAG, n_sub))
             for s in range(each):
-                relay_rows(sub(s), [s])
+                relay_rows(sub(s), [s], (lambda: own_shares(1)) if s == each - 1 else nothing)
                 if s > 0:
                     b_step(late.pop(0))
             for p in range(1, 3):
-                relay_rows(piece(p), [p * each + o for o in range(each)])
+                relay_piece(p, functools.partial(own_shares, p + 1))
                 for s in late[:2]:
                     b_step(s)
                 late = late[2:]
             for s in late:
                 b_step(s)
-            finish(0)
-            lax.fori_loop(3, n_piece - FINE, step, 0)
-            finish(n_piece - FINE - 2)
-            for s in range((n_piece - FINE) * each, n_sub):
-                relay_rows(sub(s), [s])
-            for p in range(n_piece - FINE - 1, n_piece):
+
+            def step(p, carry):
+                def between():
+                    own_shares(p + 1)
+                    finish(p - 3)
+
+                relay_piece(p, between)
+                return carry
+
+            lax.fori_loop(3, n_piece - 1, step, 0)
+            for s in range(n_sub - each, n_sub):
+                relay_rows(sub(s), [s], (lambda: finish(n_piece - 4)) if s == n_sub - each else nothing)
+            for p in range(n_piece - 3, n_piece):
                 finish(p)
 
             def drain(s, carry):
@@ -720,6 +733,7 @@
             pltpu.VMEM((tokens, channels), BF16),
         ] + [pltpu.VMEM(shape, BF16) for shape in flows] + [
             pltpu.VMEM((tokens, block), F32),
+            pltpu.VMEM((tokens, block) if relay else tiny, F32),
             dma((3, per)), dma((3,)), dma((n_chip,)), dma((n_chip,)), dma((n_chip,)),
             dma((2, 2)), dma((2, 2)), dma((2,)),
             dma((n_ctx, per)), dma((n_ctx, per)), dma((n_ctx, pieces)), dma((n_ctx, pieces)),

time: 95 us -> 94.8 us (level)
  no operation moved by 1% of the time
where the time goes in v4:
time: 94.8 us; the launch traced here: 93.8 us
  Pallas kernels  91.5 us (97%)
  local copies, waits for them, and re-layouts  2.26 us (2%)
    pallas_call x1, Pallas kernels, per_device(): pl.pallas_call(functools.partial(layer_kernel, n_ctx, n_ch, relay), out_s...  91.5 us
    unnamed x1, local copies, waits for them, and re-layouts  2.26 us

profile of v4, /device:TPU:10, one launch (start us, length us, event | category | flops | bytes accessed | tf_op | source)
XLA Modules:
  0.0 93.8 jit_solution(11953452514598255733)
XLA Ops:
  0.0 91.5 %shard_map.82 = bf16[1024,512]{1,0:T(8,128)(2,1)} custom-call(bf16[1024,512]{1,0:T(8,128)(2,1)} %q_hbm.1, bf16[1024,512]{1,0:T(8,128)(2,1)} %k_hbm.1, bf16[1024,512]{1,0:T(8,128)(2,1)} %v_hbm.1, bf16[1024,512]{1,0:T(8,128)(2,1)} %h_hbm.1, f32[1,512]{1,0:T(1,128)} %bitcast.1, bf16[2,512,256]{2,1,0:T(8,128)(2,1)} %constant.4.clone.f_hbm, ...), custom_call_target="tpu_custom_call" | custom-call | flops 8053063680 | bytes 10485760 | tf_op jit(solution)/shard_map/pallas_call | solution.py:706
  91.5 2.3 %copy.10 = bf16[1024,512]{1,0:T(8,128)(2,1)} copy(bf16[1024,512]{1,0:T(8,128)(2,1)} %shard_map.82) | data formatting | bytes 2097152

commit v5 on v4

--- a/solution.py
+++ b/solution.py
@@ -10,10 +10,10 @@
 
 BLOCK = 256
 PIECE = 128
-SUB = 64
-WINDOW = 4
-AHEAD = 2
-B_LAG = 4
+SUB = 128
+WINDOW = 3
+AHEAD = 1
+B_LAG = 2
 VMEM_MIB = 56
 F32 = jnp.float32
 BF16 = jnp.bfloat16

time: 94.8 us -> 94.2 us (level)
  no operation moved by 1% of the time
where the time goes in v5:
time: 94.2 us; the launch traced here: 93 us
  Pallas kernels  90.8 us (96%)
  local copies, waits for them, and re-layouts  2.26 us (2%)
    pallas_call x1, Pallas kernels, per_device(): pl.pallas_call(functools.partial(layer_kernel, n_ctx, n_ch, relay), out_s...  90.8 us
    unnamed x1, local copies, waits for them, and re-layouts  2.26 us

profile of v5, /device:TPU:10, one launch (start us, length us, event | category | flops | bytes accessed | tf_op | source)
XLA Modules:
  0.0 93.0 jit_solution(1480862340156164296)
XLA Ops:
  0.0 90.8 %shard_map.82 = bf16[1024,512]{1,0:T(8,128)(2,1)} custom-call(bf16[1024,512]{1,0:T(8,128)(2,1)} %q_hbm.1, bf16[1024,512]{1,0:T(8,128)(2,1)} %k_hbm.1, bf16[1024,512]{1,0:T(8,128)(2,1)} %v_hbm.1, bf16[1024,512]{1,0:T(8,128)(2,1)} %h_hbm.1, f32[1,512]{1,0:T(1,128)} %bitcast.1, bf16[2,512,256]{2,1,0:T(8,128)(2,1)} %constant.4.clone.f_hbm, ...), custom_call_target="tpu_custom_call" | custom-call | flops 8053063680 | bytes 10485760 | tf_op jit(solution)/shard_map/pallas_call | solution.py:706
  90.8 2.3 %copy.10 = bf16[1024,512]{1,0:T(8,128)(2,1)} copy(bf16[1024,512]{1,0:T(8,128)(2,1)} %shard_map.82) | data formatting | bytes 2097152
